TPU v7x, 512 devices: a whole 4x4x16 slice. The times are simulated.
512 devices in a mesh: row: 8 (over y, z_hi), col: 64 (over z_lo, x, core).
Axes of the slice: x: 4, y: 4, z: 16 (z_hi: 2, z_lo: 8; z = z_hi * 8 + z_lo), core: 2. Of those that a mesh axis runs over, the one named last changes fastest.
Arguments:
- side_a: float32 [64, 8192], P('row', 'col'), may hold values from -6 to 6
- side_b: float32 [2048, 8192], P('col', 'row'), may hold values from -6 to 6
- pair_grad: float32 [64, 2048, 128], P('row', 'col'), may hold values from -6 to 6
- out_weight: float32 [1024, 128], replicated, may hold values from -0.1875 to 0.1875
Outputs:
- grad_a: float32 [64, 8192], P('row', 'col')
- grad_b: float32 [2048, 8192], P('col', 'row')
- grad_weight: float32 [1024, 128], replicated
- grad_bias: float32 [128], replicated
All inputs are finite; a program needn't handle non-finite values.
Results may differ from a plain program's by a relative error of at most 0.00013.
Values sent between devices are 32-bit elements; how exact they have to be, the bound alone decides.
A program may use at most 64 MiB of HBM per device.

v0:
```python
import jax
import jax.numpy as jnp
from jax import lax
from jax.sharding import PartitionSpec as P

S = 256
C = 32
P_SIZE = 128


def local(side_a, side_b, pair_grad, out_weight):
    high = lax.Precision.HIGHEST
    rows = pair_grad.shape[0]
    cols = pair_grad.shape[1]
    left = lax.all_gather(side_a, "col", axis=1, tiled=True).reshape(rows, S, C)
    right = lax.all_gather(side_b, "row", axis=1, tiled=True).reshape(cols, S, C)
    left_flat = jnp.transpose(left, (0, 2, 1)).reshape(rows * C, S)
    right_flat = jnp.transpose(right, (1, 0, 2)).reshape(S, cols * C)
    flat_pair = pair_grad.reshape(rows * cols, P_SIZE)
    grad_outer = jnp.dot(flat_pair, out_weight.T, precision=high)
    grad_tile = jnp.transpose(grad_outer.reshape(rows, cols, C, C), (0, 2, 1, 3)).reshape(
        rows * C, cols * C
    )
    left_grad = jnp.dot(grad_tile, right_flat.T, precision=high) / S
    left_part = jnp.transpose(left_grad.reshape(rows, C, S), (0, 2, 1)).reshape(rows, S * C)
    right_grad = jnp.dot(left_flat.T, grad_tile, precision=high) / S
    right_part = jnp.transpose(right_grad.reshape(S, cols, C), (1, 0, 2)).reshape(cols, S * C)
    left_total = lax.psum(left_part, "col")
    right_total = lax.psum(right_part, "row")
    left_width = side_a.shape[1]
    right_width = side_b.shape[1]
    grad_a = lax.dynamic_slice_in_dim(left_total, lax.axis_index("col") * left_width, left_width, 1)
    grad_b = lax.dynamic_slice_in_dim(
        right_total, lax.axis_index("row") * right_width, right_width, 1
    )
    outer = jnp.dot(left_flat, right_flat, precision=high) / S
    outer = jnp.transpose(outer.reshape(rows, C, cols, C), (0, 2, 1, 3)).reshape(rows * cols, C * C)
    weight_part = jnp.dot(outer.T, flat_pair, precision=high)
    bias_part = jnp.sum(flat_pair, axis=0)
    weight_sums = lax.psum((weight_part, bias_part), ("row", "col"))
    return (grad_a, grad_b, weight_sums[0], weight_sums[1])


def solution(mesh):
    in_specs = (P("row", "col"), P("col", "row"), P("row", "col", None), P())
    out_specs = (P("row", "col"), P("col", "row"), P(), P())
    return jax.shard_map(local, mesh=mesh, in_specs=in_specs, out_specs=out_specs, check_vma=False)
```

profile of v0, /device:TPU:4, one launch (start us, length us, event | category | flops | bytes accessed | tf_op | source)
XLA Modules:
  0.0 1648.9 jit_solution(14450162567662222692)
XLA Ops:
  7.2 0.0 copy-start
  7.2 0.0 all-gather.2.cloned.1.call-start
  7.2 0.7 all-gather.2.cloned.1.call-update
  7.9 0.0 all-reduce.6.cloned.1.call-start
  8.0 0.3 copy-done
  8.2 0.0 copy-start.2
  8.2 5.9 convolution_bitcast_fusion
  14.1 3.7 reshape.48
  17.9 0.0 copy-done.2
  17.9 119.1 %all_gather.7 = f32[8,8192]{1,0:T(8,128)S(1)} all-gather(f32[8,128]{1,0:T(8,128)S(1)} %copy-done.2), channel_id=1, replica_groups=mesh['row'=8,'col'=64] {'col'}, dimensions={1}, use_global_device_ids=true | all-gather | bytes 266240 | tf_op jit(solution)/shard_map/all_gather | solution.py:15
  137.0 0.3 reshape.53
  137.3 0.3 copy.12
  137.6 1.8 convolution_multiply_fusion.1
  139.5 2.6 copy.13
  142.1 4.4 reshape.56
  146.5 0.0 all-reduce.6.cloned.1.call-update
  146.5 0.2 all-reduce.4.cloned.1.call-start
  146.8 0.0 all-gather.2.cloned.1.call-done
  146.8 3.7 reshape.49
  150.5 2.8 copy.10
  153.3 1.0 convolution_multiply_fusion.2
  154.4 0.3 copy.11
  154.7 1.2 reshape.52
  155.9 1.0 convolution_multiply_fusion
  157.0 2.7 reshape.57
  159.7 6.5 copy.17
  166.2 0.0 copy-start.1
  166.2 3.8 reshape.58
  170.0 0.0 all-reduce.4.cloned.1.call-update
  170.0 0.0 all-reduce.8.cloned.1.call-start
  170.1 0.0 copy-done.1
  170.1 2.6 fusion.1
  172.7 0.0 all-reduce.8.cloned.1.call-update
  172.7 0.1 reduce_sum.9
  172.8 158.6 %psum.31 = f32[128]{0:T(128)} all-reduce(f32[128]{0:T(128)S(1)} %reduce_sum.9), channel_id=1, replica_groups=mesh['row'=8,'col'=64] {'row','col'}, use_global_device_ids=true, to_apply=%region_4.0 | all-reduce | flops 128 | bytes 1024 | tf_op jit(solution)/shard_map/psum | solution.py:40
  331.4 64.2 %all-reduce.6.cloned.1.call-done = f32[32,8192]{1,0:T(8,128)} async-done(((f32[32,8192]{1,0:T(8,128)}), f32[32,8192]{1,0:T(8,128)}) %all-reduce.6.cloned.1.call-update) | async-done | bytes 1048592 | tf_op jit(solution)/shard_map/psum | solution.py:29
  395.6 1.6 constant_dynamic-slice_fusion
  397.2 767.8 %all-reduce.4.cloned.1.call-done = f32[8,8192]{1,0:T(8,128)} async-done(((f32[8,8192]{1,0:T(8,128)}), f32[8,8192]{1,0:T(8,128)}) %all-reduce.4.cloned.1.call-update) | async-done | bytes 262160 | tf_op jit(solution)/shard_map/psum | solution.py:28
  1165.0 1.3 constant_dynamic-slice_fusion.1
  1166.3 474.2 %all-reduce.8.cloned.1.call-done = f32[1024,128]{1,0:T(8,128)} async-done(((f32[1024,128]{1,0:T(8,128)}), f32[1024,128]{1,0:T(8,128)}) %all-reduce.8.cloned.1.call-update) | async-done | bytes 524304 | tf_op jit(solution)/shard_map/psum | solution.py:40
  1640.5 1.9 copy.21
Async XLA Ops:
  7.2 1.0 copy-start
  7.2 139.6 %all-gather.2.cloned.1.call-start = ((), (), s32[]{:S(2)}) async-start(), calls=%async_computation | async-start | bytes 1179648 | tf_op jit(solution)/shard_map/all_gather | solution.py:16
  7.9 387.7 %all-reduce.6.cloned.1.call-start = ((), (), s32[]{:S(2)}) async-start(), calls=%async_computation.2 | async-start | bytes 2097152 | tf_op jit(solution)/shard_map/psum | solution.py:29
  8.2 9.7 copy-start.2
  146.5 1018.5 %all-reduce.4.cloned.1.call-start = ((), (), s32[]{:S(2)}) async-start(), calls=%async_computation.1 | async-start | bytes 524288 | tf_op jit(solution)/shard_map/psum | solution.py:28
  166.2 3.9 copy-start.1
  170.0 1470.4 %all-reduce.8.cloned.1.call-start = ((), (), s32[]{:S(2)}) async-start(), calls=%async_computation.3 | async-start | bytes 1048576 | tf_op jit(solution)/shard_map/psum | solution.py:40
Sparse Core Ops, SparseCore 0:
  11.2 95.5 all-gather.1
  146.6 248.9 all-reduce.5
  398.5 766.4 all-reduce.3
  1171.8 468.6 all-reduce.7
where the time goes:
time: 1650 us
  waiting for transfers between devices  1310 us (79%)
  blocking collectives  278 us (17%)
  local copies, waits for them, and re-layouts  37.5 us (2%)
    psum x1, waiting for transfers between devices, local(): left_total = lax.psum(left_part, 'col')  768 us
    psum x1, waiting for transfers between devices, local(): weight_sums = lax.psum((weight_part, bias_part), ('row', 'col'))  474 us
    psum x1, blocking collectives, local(): weight_sums = lax.psum((weight_part, bias_part), ('row', 'col'))  159 us
    all_gather x1, blocking collectives, local(): left = lax.all_gather(side_a, 'col', axis=1, tiled=True).reshape(rows, S, C)  119 us
    psum x1, waiting for transfers between devices, local(): right_total = lax.psum(right_part, 'row')  64.2 us
  transfers between devices with their start and end apart: 4, of which 3 were waited for; matrix products, arithmetic and copies ran while one was open for 3% of the time, Pallas kernels for 0%

commit v1 on v0

--- a/solution.py
+++ b/solution.py
@@ -37,7 +37,7 @@
     outer = jnp.transpose(outer.reshape(rows, C, cols, C), (0, 2, 1, 3)).reshape(rows * cols, C * C)
     weight_part = jnp.dot(outer.T, flat_pair, precision=high)
     bias_part = jnp.sum(flat_pair, axis=0)
-    weight_sums = lax.psum((weight_part, bias_part), ("row", "col"))
+    weight_sums = lax.psum(lax.psum((weight_part, bias_part), "col"), "row")
     return (grad_a, grad_b, weight_sums[0], weight_sums[1])
 
 

time: 1650 us -> 1320 us (0.80)
  the two profiles are of different devices: /device:TPU:4 before, /device:TPU:1 now
where the time goes in v1:
time: 1320 us
  waiting for transfers between devices  794 us (60%)
  blocking collectives  455 us (34%)
  local copies, waits for them, and re-layouts  39.2 us (3%)
  matrix products  14.6 us (1%)
  between operations  13.8 us (1%)
    psum x1, waiting for transfers between devices, local(): left_total = lax.psum(left_part, 'col')  793 us
    psum x2, blocking collectives, local(): weight_sums = lax.psum(lax.psum((weight_part, bias_part), 'col'), 'row')  317 us
    all_gather x1, blocking collectives, local(): left = lax.all_gather(side_a, 'col', axis=1, tiled=True).reshape(rows, S, C)  137 us
  transfers between devices with their start and end apart: 3, of which 1 were waited for; matrix products, arithmetic and copies ran while one was open for 2% of the time, Pallas kernels for 0%

profile of v1, /device:TPU:1, one launch (start us, length us, event | category | flops | bytes accessed | tf_op | source)
XLA Modules:
  0.0 1316.5 jit_solution(12140611257966285544)
XLA Ops:
  7.2 0.0 copy-start
  7.2 0.0 all-gather.2.cloned.1.call-start
  7.2 0.7 all-gather.2.cloned.1.call-update
  7.9 0.0 all-reduce.5.cloned.1.call-start
  8.0 137.4 %all_gather.7 = f32[8,8192]{1,0:T(8,128)S(1)} all-gather(f32[8,128]{1,0:T(8,128)} %param.4), channel_id=1, replica_groups=mesh['row'=8,'col'=64] {'col'}, dimensions={1}, use_global_device_ids=true | all-gather | bytes 266240 | tf_op jit(solution)/shard_map/all_gather | solution.py:15
  145.3 0.3 reshape.53
  145.7 0.3 copy.12
  146.0 0.0 copy-done
  146.0 5.9 convolution_bitcast_fusion
  151.9 3.7 reshape.48
  155.7 0.0 all-gather.2.cloned.1.call-done
  155.7 3.7 reshape.49
  159.4 2.8 copy.10
  162.2 2.0 convolution_multiply_fusion
  164.3 3.9 reshape.57
  168.2 6.5 copy.17
  174.7 0.0 copy-start.1
  174.7 4.6 reshape.58
  179.3 1.0 convolution_multiply_fusion.2
  180.3 0.3 copy.11
  180.7 1.2 reshape.52
  181.9 0.0 copy-done.1
  181.9 3.8 fusion.1
  185.7 0.0 all-reduce.5.cloned.1.call-update
  185.8 0.0 all-reduce.7.cloned.1.call-start
  185.8 1.8 convolution_multiply_fusion.1
  187.6 2.6 copy.13
  190.3 4.3 reshape.56
  194.6 793.2 %all-reduce.5.cloned.1.call-done = (f32[8,8192]{1,0:T(8,128)}, f32[1024,128]{1,0:T(8,128)}) async-done(((f32[8,8192]{1,0:T(8,128)}, f32[1024,128]{1,0:T(8,128)}), (f32[8,8192]{1,0:T(8,128)}, f32[1024,128]{1,0:T(8,128)})) %all-reduce.5.cloned.1.call-update) | async-done | bytes 786448 | tf_op jit(solution)/shard_map/psum | solution.py:28
  987.8 0.0 all-reduce.7.cloned.1.call-update
  987.8 0.1 reduce_sum.9
  987.9 259.9 %psum.46 = f32[128]{0:T(128)S(1)} all-reduce(f32[128]{0:T(128)S(1)} %reduce_sum.9), channel_id=1, replica_groups=mesh['row'=8,'col'=64] {'col'}, use_global_device_ids=true, to_apply=%region_5.0 | all-reduce | flops 128 | bytes 1024 | tf_op jit(solution)/shard_map/psum | solution.py:40
  1247.8 57.5 %psum.47 = f32[128]{0:T(128)} all-reduce(f32[128]{0:T(128)S(1)} %psum.46), channel_id=1, replica_groups=mesh['row'=8,'col'=64] {'row'}, use_global_device_ids=true, to_apply=%region_6.0 | all-reduce | flops 128 | bytes 1024 | tf_op jit(solution)/shard_map/psum | solution.py:40
  1305.3 1.3 constant_dynamic-slice_fusion.1
  1306.5 0.0 all-reduce.7.cloned.1.call-done
  1306.5 1.6 constant_dynamic-slice_fusion
  1308.1 1.9 copy.22
Async XLA Ops:
  7.2 138.8 %copy-start = (f32[1024,128]{1,0:T(8,128)S(1)}, f32[1024,128]{1,0:T(8,128)}, u32[]{:S(2)}) copy-start(f32[1024,128]{1,0:T(8,128)} %param.7) | copy-start | bytes 1572868
  7.2 148.5 %all-gather.2.cloned.1.call-start = ((), (), s32[]{:S(2)}) async-start(), calls=%async_computation | async-start | bytes 1179648 | tf_op jit(solution)/shard_map/all_gather | solution.py:16
  7.9 979.9 %all-reduce.5.cloned.1.call-start = ((), (), s32[]{:S(2)}) async-start(), calls=%async_computation.1 | async-start | bytes 1572864 | tf_op jit(solution)/shard_map/psum | solution.py:28
  174.7 7.2 copy-start.1
  185.8 1120.8 %all-reduce.7.cloned.1.call-start = ((), (), s32[]{:S(2)}) async-start(), calls=%async_computation.2 | async-start | bytes 3145728 | tf_op jit(solution)/shard_map/psum | solution.py:29
Sparse Core Ops, SparseCore 0:
  11.2 95.2 all-gather.1
  185.9 801.8 all-reduce.4
  991.1 307.4 all-reduce.6

commit v2 on v0

--- a/solution.py
+++ b/solution.py
@@ -12,7 +12,9 @@
     high = lax.Precision.HIGHEST
     rows = pair_grad.shape[0]
     cols = pair_grad.shape[1]
-    left = lax.all_gather(side_a, "col", axis=1, tiled=True).reshape(rows, S, C)
+    left = jnp.concatenate(
+        lax.all_to_all(jnp.stack([side_a] * lax.axis_size("col")), "col", 0, 0), axis=1
+    ).reshape(rows, S, C)
     right = lax.all_gather(side_b, "row", axis=1, tiled=True).reshape(cols, S, C)
     left_flat = jnp.transpose(left, (0, 2, 1)).reshape(rows * C, S)
     right_flat = jnp.transpose(right, (1, 0, 2)).reshape(S, cols * C)

time: 1650 us -> 1590 us (0.964)
  blocking collectives: 278 us -> 133 us
  waiting for transfers between devices: 1310 us -> 1370 us
    all_gather x1 -> x0, blocking collectives: 119 us -> none  [local(): left = lax.all_gather(side_a, 'col', axis=1, tiled=True).reshape(rows, S, C)]
    all_gather x1, waiting for transfers between devices: 0.02 us -> 57.1 us  [local(): lax.all_gather(side_b, 'row', axis=1, tiled=True).reshape(cols, S, C)]
    psum x1, blocking collectives: 159 us -> 133 us  [local(): weight_sums = lax.psum((weight_part, bias_part), ('row', 'col'))]
  transfers between devices with their start and end apart: 4 -> 5, of which waited for: 3 -> 5; matrix products, arithmetic and copies ran while one was open for 3% -> 3% of each run, Pallas kernels for 0% -> 0%
where the time goes in v2:
time: 1590 us
  waiting for transfers between devices  1370 us (86%)
  blocking collectives  133 us (8%)
  local copies, waits for them, and re-layouts  38.6 us (2%)
  starting transfers between devices  16.4 us (1%)
    psum x1, waiting for transfers between devices, local(): left_total = lax.psum(left_part, 'col')  771 us
    psum x1, waiting for transfers between devices, local(): weight_sums = lax.psum((weight_part, bias_part), ('row', 'col'))  474 us
    psum x1, blocking collectives, local(): weight_sums = lax.psum((weight_part, bias_part), ('row', 'col'))  133 us
    psum x1, waiting for transfers between devices, local(): right_total = lax.psum(right_part, 'row')  60.8 us
    all_gather x1, waiting for transfers between devices, local(): lax.all_gather(side_b, 'row', axis=1, tiled=True).reshape(cols, S, C)  57.1 us
  transfers between devices with their start and end apart: 5, of which 5 were waited for; matrix products, arithmetic and copies ran while one was open for 3% of the time, Pallas kernels for 0%

profile of v2, /device:TPU:4, one launch (start us, length us, event | category | flops | bytes accessed | tf_op | source)
XLA Modules:
  0.0 1586.4 jit_solution(7640439222442611940)
XLA Ops:
  7.2 0.0 copy-start
  7.2 0.0 all-gather.2.cloned.1.call-start
  7.2 0.7 all-gather.2.cloned.1.call-update
  7.9 1.4 stack.2
  9.3 16.0 %all-to-all-start = ((f32[64,8,128]{2,1,0:T(8,128)}), f32[64,8,128]{2,1,0:T(8,128)S(1)}, u32[]{:S(2)}, u32[]{:S(2)}) async-start(f32[64,8,128]{2,1,0:T(8,128)} %stack.2), calls=%async_computation | async-start | bytes 524288 | tf_op jit(solution)/shard_map/all_to_all | solution.py:16
  25.4 0.0 all-reduce.6.cloned.1.call-start
  25.4 0.0 copy-done
  25.4 5.9 convolution_bitcast_fusion
  31.4 3.8 reshape.50
  35.2 8.0 all-to-all-done
  43.2 0.1 copy.17
  43.2 0.3 reshape_reshape.3
  43.5 0.3 copy.18
  43.8 1.8 convolution_multiply_fusion.1
  45.6 2.6 copy.19
  48.3 4.4 reshape.58
  52.6 0.0 all-reduce.6.cloned.1.call-update
  52.7 0.2 all-reduce.4.cloned.1.call-start
  52.9 57.1 %all-gather.2.cloned.1.call-done = f32[32,8192]{1,0:T(8,128)} async-done(((f32[32,1024]{1,0:T(8,128)}), f32[32,8192]{1,0:T(8,128)}) %all-gather.2.cloned.1.call-update) | async-done | bytes 1048592 | tf_op jit(solution)/shard_map/all_gather | solution.py:18
  110.0 3.7 reshape.51
  113.7 2.8 copy.15
  116.5 1.0 convolution_multiply_fusion.2
  117.5 0.3 copy.16
  117.9 1.2 reshape.54
  119.1 1.0 convolution_multiply_fusion
  120.1 2.7 reshape.59
  122.8 6.5 copy.23
  129.4 0.0 copy-start.1
  129.4 3.8 reshape.60
  133.2 0.0 all-reduce.4.cloned.1.call-update
  133.2 0.0 all-reduce.8.cloned.1.call-start
  133.2 0.0 copy-done.1
  133.2 2.6 fusion.1
  135.9 0.0 all-reduce.8.cloned.1.call-update
  135.9 0.1 reduce_sum.9
  135.9 133.3 %psum.31 = f32[128]{0:T(128)} all-reduce(f32[128]{0:T(128)S(1)} %reduce_sum.9), channel_id=1, replica_groups=mesh['row'=8,'col'=64] {'row','col'}, use_global_device_ids=true, to_apply=%region_4.0 | all-reduce | flops 128 | bytes 1024 | tf_op jit(solution)/shard_map/psum | solution.py:42
  269.2 60.8 %all-reduce.6.cloned.1.call-done = f32[32,8192]{1,0:T(8,128)} async-done(((f32[32,8192]{1,0:T(8,128)}), f32[32,8192]{1,0:T(8,128)}) %all-reduce.6.cloned.1.call-update) | async-done | bytes 1048592 | tf_op jit(solution)/shard_map/psum | solution.py:31
  329.9 1.6 constant_dynamic-slice_fusion
  331.5 771.0 %all-reduce.4.cloned.1.call-done = f32[8,8192]{1,0:T(8,128)} async-done(((f32[8,8192]{1,0:T(8,128)}), f32[8,8192]{1,0:T(8,128)}) %all-reduce.4.cloned.1.call-update) | async-done | bytes 262160 | tf_op jit(solution)/shard_map/psum | solution.py:30
  1102.5 1.3 constant_dynamic-slice_fusion.1
  1103.8 474.2 %all-reduce.8.cloned.1.call-done = f32[1024,128]{1,0:T(8,128)} async-done(((f32[1024,128]{1,0:T(8,128)}), f32[1024,128]{1,0:T(8,128)}) %all-reduce.8.cloned.1.call-update) | async-done | bytes 524304 | tf_op jit(solution)/shard_map/psum | solution.py:42
  1578.0 1.9 copy.27
Async XLA Ops:
  7.2 18.3 %copy-start = (f32[1024,128]{1,0:T(8,128)S(1)}, f32[1024,128]{1,0:T(8,128)}, u32[]{:S(2)}) copy-start(f32[1024,128]{1,0:T(8,128)} %param.7) | copy-start | bytes 1572868
  7.2 102.8 %all-gather.2.cloned.1.call-start = ((), (), s32[]{:S(2)}) async-start(), calls=%async_computation.1 | async-start | bytes 1179648 | tf_op jit(solution)/shard_map/all_gather | solution.py:18
  9.3 33.8 %all-to-all-start = ((f32[64,8,128]{2,1,0:T(8,128)}), f32[64,8,128]{2,1,0:T(8,128)S(1)}, u32[]{:S(2)}, u32[]{:S(2)}) async-start(f32[64,8,128]{2,1,0:T(8,128)} %stack.2), calls=%async_computation | async-start | bytes 524288 | tf_op jit(solution)/shard_map/all_to_all | solution.py:16
  25.4 304.6 %all-reduce.6.cloned.1.call-start = ((), (), s32[]{:S(2)}) async-start(), calls=%async_computation.3 | async-start | bytes 2097152 | tf_op jit(solution)/shard_map/psum | solution.py:31
  52.7 1049.9 %all-reduce.4.cloned.1.call-start = ((), (), s32[]{:S(2)}) async-start(), calls=%async_computation.2 | async-start | bytes 524288 | tf_op jit(solution)/shard_map/psum | solution.py:30
  129.4 3.9 copy-start.1
  133.2 1444.8 %all-reduce.8.cloned.1.call-start = ((), (), s32[]{:S(2)}) async-start(), calls=%async_computation.4 | async-start | bytes 1048576 | tf_op jit(solution)/shard_map/psum | solution.py:42
Sparse Core Ops, SparseCore 0:
  11.2 98.6 all-gather.1
  112.9 216.9 all-reduce.5
  332.9 769.6 all-reduce.3
  1109.3 468.6 all-reduce.7

commit v3 on v0

--- a/solution.py
+++ b/solution.py
@@ -25,7 +25,7 @@
     left_part = jnp.transpose(left_grad.reshape(rows, C, S), (0, 2, 1)).reshape(rows, S * C)
     right_grad = jnp.dot(left_flat.T, grad_tile, precision=high) / S
     right_part = jnp.transpose(right_grad.reshape(S, cols, C), (1, 0, 2)).reshape(cols, S * C)
-    left_total = lax.psum(left_part, "col")
+    left_total = jnp.sum(lax.all_gather(left_part, "col"), axis=0)
     right_total = lax.psum(right_part, "row")
     left_width = side_a.shape[1]
     right_width = side_b.shape[1]

time: 1650 us -> 1000 us (0.61)
  waiting for transfers between devices: 1310 us -> 652 us
    psum x1 -> x0, waiting for transfers between devices: 768 us -> none  [local(): left_total = lax.psum(left_part, 'col')]
    all_gather x0 -> x1, waiting for transfers between devices: none -> 135 us  [local(): left_total = jnp.sum(lax.all_gather(left_part, 'col'), axis=0)]
    psum x1, waiting for transfers between devices: 474 us -> 455 us  [local(): weight_sums = lax.psum((weight_part, bias_part), ('row', 'col'))]
  transfers between devices with their start and end apart: 4 -> 4, of which waited for: 3 -> 3; matrix products, arithmetic and copies ran while one was open for 3% -> 5% of each run, Pallas kernels for 0% -> 0%
where the time goes in v3:
time: 1000 us
  waiting for transfers between devices  652 us (65%)
  blocking collectives  278 us (28%)
  local copies, waits for them, and re-layouts  36.8 us (4%)
  between operations  13.9 us (1%)
  matrix products  12.4 us (1%)
    psum x1, waiting for transfers between devices, local(): weight_sums = lax.psum((weight_part, bias_part), ('row', 'col'))  455 us
    psum x1, blocking collectives, local(): weight_sums = lax.psum((weight_part, bias_part), ('row', 'col'))  159 us
    all_gather x1, waiting for transfers between devices, local(): left_total = jnp.sum(lax.all_gather(left_part, 'col'), axis=0)  135 us
    all_gather x1, blocking collectives, local(): left = lax.all_gather(side_a, 'col', axis=1, tiled=True).reshape(rows, S, C)  119 us
    psum x1, waiting for transfers between devices, local(): right_total = lax.psum(right_part, 'row')  61.9 us
  transfers between devices with their start and end apart: 4, of which 3 were waited for; matrix products, arithmetic and copies ran while one was open for 5% of the time, Pallas kernels for 0%

profile of v3, /device:TPU:4, one launch (start us, length us, event | category | flops | bytes accessed | tf_op | source)
XLA Modules:
  0.0 1000.8 jit_solution(6339201219841638219)
XLA Ops:
  7.2 0.0 copy-start
  7.2 0.0 all-gather.3.cloned.1.call-start
  7.2 0.7 all-gather.3.cloned.1.call-update
  7.9 0.0 all-reduce.3.cloned.1.call-start
  8.0 0.3 copy-done
  8.2 0.0 copy-start.2
  8.2 5.9 convolution_bitcast_fusion
  14.1 3.7 reshape.45
  17.9 0.0 copy-done.2
  17.9 119.1 %all_gather.11 = f32[8,8192]{1,0:T(8,128)S(1)} all-gather(f32[8,128]{1,0:T(8,128)S(1)} %copy-done.2), channel_id=1, replica_groups=mesh['row'=8,'col'=64] {'col'}, dimensions={1}, use_global_device_ids=true | all-gather | bytes 266240 | tf_op jit(solution)/shard_map/all_gather | solution.py:15
  137.0 0.3 reshape.49
  137.3 0.3 copy.16
  137.6 1.8 convolution_multiply_fusion.1
  139.5 2.6 copy.17
  142.1 4.4 reshape.52
  146.5 0.0 all-reduce.3.cloned.1.call-update
  146.5 0.0 all-gather.5.cloned.1.call-start
  146.6 0.0 all-gather.3.cloned.1.call-done
  146.6 3.7 reshape.46
  150.3 2.8 copy.14
  153.1 1.0 convolution_multiply_fusion.2
  154.2 0.3 copy.15
  154.5 1.2 all_gather_reshape.3
  155.7 0.0 all-gather.5.cloned.1.call-update
  155.8 0.2 all-reduce.5.cloned.1.call-start
  156.0 1.0 convolution_multiply_fusion
  157.1 2.7 reshape.53
  159.8 6.5 copy.21
  166.3 0.0 copy-start.1
  166.3 3.8 reshape.54
  170.1 0.0 copy-done.1
  170.1 2.6 fusion.1
  172.7 0.0 all-reduce.5.cloned.1.call-update
  172.7 0.1 reduce_sum.19
  172.8 159.4 %psum.23 = f32[128]{0:T(128)} all-reduce(f32[128]{0:T(128)S(1)} %reduce_sum.19), channel_id=1, replica_groups=mesh['row'=8,'col'=64] {'row','col'}, use_global_device_ids=true, to_apply=%region_4.0 | all-reduce | flops 128 | bytes 1024 | tf_op jit(solution)/shard_map/psum | solution.py:40
  332.2 61.9 %all-reduce.3.cloned.1.call-done = f32[32,8192]{1,0:T(8,128)} async-done(((f32[32,8192]{1,0:T(8,128)}), f32[32,8192]{1,0:T(8,128)}) %all-reduce.3.cloned.1.call-update) | async-done | bytes 1048592 | tf_op jit(solution)/shard_map/psum | solution.py:29
  394.1 1.6 constant_dynamic-slice_fusion
  395.6 134.9 %all-gather.5.cloned.1.call-done = f32[64,8,8192]{2,1,0:T(8,128)} async-done(((f32[1,8,8192]{2,1,0:T(8,128)}), f32[64,8,8192]{2,1,0:T(8,128)}) %all-gather.5.cloned.1.call-update) | async-done | bytes 16777232 | tf_op jit(solution)/shard_map/all_gather | solution.py:28
  530.6 6.5 reduce_sum.18
  537.1 0.6 constant_dynamic-slice_fusion.1
  537.7 454.7 %all-reduce.5.cloned.1.call-done = f32[1024,128]{1,0:T(8,128)} async-done(((f32[1024,128]{1,0:T(8,128)}), f32[1024,128]{1,0:T(8,128)}) %all-reduce.5.cloned.1.call-update) | async-done | bytes 524304 | tf_op jit(solution)/shard_map/psum | solution.py:40
  992.4 1.9 copy.24
Async XLA Ops:
  7.2 1.0 copy-start
  7.2 139.4 %all-gather.3.cloned.1.call-start = ((), (), s32[]{:S(2)}) async-start(), calls=%async_computation | async-start | bytes 1179648 | tf_op jit(solution)/shard_map/all_gather | solution.py:16
  7.9 386.2 %all-reduce.3.cloned.1.call-start = ((), (), s32[]{:S(2)}) async-start(), calls=%async_computation.2 | async-start | bytes 2097152 | tf_op jit(solution)/shard_map/psum | solution.py:29
  8.2 9.7 copy-start.2
  146.5 384.1 %all-gather.5.cloned.1.call-start = ((), (), s32[]{:S(2)}) async-start(), calls=%async_computation.1 | async-start | bytes 17039360 | tf_op jit(solution)/shard_map/all_gather | solution.py:28
  155.8 836.7 %all-reduce.5.cloned.1.call-start = ((), (), s32[]{:S(2)}) async-start(), calls=%async_computation.3 | async-start | bytes 1048576 | tf_op jit(solution)/shard_map/psum | solution.py:40
  166.3 3.8 copy-start.1
Sparse Core Ops, SparseCore 0:
  11.2 95.5 all-gather.2
  146.6 247.3 all-reduce.2
  396.2 134.2 all-gather.4
  536.5 455.9 all-reduce.4
